TPU v7x, 32 devices: a whole 2x2x4 slice. The times are simulated.
32 devices in a mesh: gx: 2 (over core), gy: 4 (over y, x), gz: 4 (over z).
Axes of the slice: x: 2, y: 2, z: 4, core: 2. Of those that a mesh axis runs over, the one named last changes fastest.
Arguments:
- velocity: float32 [3, 128, 64, 512], P(None, 'gx', 'gy', 'gz'), may hold values from -6 to 6
- viscosity: float32 [128, 64, 512], P('gx', 'gy', 'gz'), may hold values from 0.01 to 0.3
- point_force: float32 [3, 32768], P(None, ('gx', 'gy', 'gz')), may hold values from -300 to 300
- point_offset: float32 [3, 32768], P(None, ('gx', 'gy', 'gz')), may hold values from 0 to 1
- point_cell: int32 [32768], P(('gx', 'gy', 'gz')), may hold values from 0 to 131071, as said below
- point_tile: int32 [32768, 1], P(('gx', 'gy', 'gz')), may hold values from 0 to 31, as said below
Outputs:
- new_velocity: float32 [3, 128, 64, 512], P(None, 'gx', 'gy', 'gz')
- point_velocity: float32 [3, 32768], P(None, ('gx', 'gy', 'gz'))
Inputs may be any that keep to these rules, and one draw needn't show every extreme that they name: `point_tile`: the 1024 points of one device form 8 runs of 128 points in a row; each run names one tile, the 8 tiles of a device differ, the first is the device's own tile and the others differ from it by at most one in each of the three tile coordinates. `point_cell`: the cell's flat index (i * 16 + j) * 128 + k within its tile.
All inputs are finite; a program needn't handle non-finite values.
Results may differ from a plain program's by a relative error of at most 0.0003.
Values sent between devices are 32-bit elements; how exact they have to be, the bound alone decides.
A program may use at most 64 MiB of HBM per device.

v0:
```python
import functools

import jax
import jax.numpy as jnp
from jax import lax
from jax.experimental import pallas as pl
from jax.experimental.pallas import tpu as pltpu
from jax.sharding import PartitionSpec as P

MESH = pl.DeviceIdType.MESH
time_step = 0.1
kernel_width = 2.0
one_third = 1.0 / 3.0
two_thirds = 2.0 / 3.0
run_count = 8


def split_by(x, n):
    if n & (n - 1) == 0:
        bits = n.bit_length() - 1
        return lax.shift_right_logical(x, jnp.int32(bits)), x & (n - 1)
    return lax.div(x, jnp.int32(n)), lax.rem(x, jnp.int32(n))


def halves(x):
    high = x.astype(jnp.bfloat16)
    low = (x - high.astype(jnp.float32)).astype(jnp.bfloat16)
    return high, low


def weights(centre, cells):
    middles = lax.broadcasted_iota(jnp.int32, (cells, centre.shape[1]), 0).astype(jnp.float32) + 0.5
    scaled = (middles - centre) / kernel_width
    unscaled = jnp.exp(-scaled * scaled)
    return unscaled / jnp.sum(unscaled, axis=0, keepdims=True)


def kernel(
    sizes,
    vel,
    visc,
    force,
    offset,
    cell,
    tile,
    out_vel,
    out_pts,
    field,
    force_acc,
    forcing,
    w_high,
    w_low,
    product,
    v_split,
    vals,
    neighbour,
    pay,
    slots,
    sampled,
    returned,
    y_send,
    y_recv,
    z_send,
    z_recv,
    z_mix,
    pay_ss,
    pay_rs,
    ret_ss,
    ret_rs,
    x_ss,
    x_rs,
    y_ss,
    y_rs,
    z_ss,
    z_rs,
):
    (na, nb, nc), (cx, cy, cz), cap = sizes
    a, b, c = (lax.axis_index(axis) for axis in ("gx", "gy", "gz"))
    where_am_i = (a, b, c)
    counts = (na, nb, nc)
    half_planes = cx // 2
    groups = half_planes // 4

    def step_of(n):
        return n // 9 - 1, n // 3 % 3 - 1, n % 3 - 1

    def inside(place):
        ok = (place[0] >= 0) & (place[0] < na)
        ok &= (place[1] >= 0) & (place[1] < nb)
        return ok & (place[2] >= 0) & (place[2] < nc)

    def target_of(n, sign):
        da, db, dc = step_of(n)
        return a + sign * da, b + sign * db, c + sign * dc

    slots[...] = jnp.zeros_like(slots)
    returned[...] = jnp.zeros_like(returned)
    y_recv[...] = jnp.zeros_like(y_recv)
    z_recv[...] = jnp.zeros_like(z_recv)
    edge = jnp.zeros((3, 2) + field.shape[3:], jnp.float32)
    for s in range(3):
        field[s, :, 0:2] = edge
        field[s, :, cx + 2 : cx + 4] = edge

    barrier = pltpu.get_barrier_semaphore()

    def greet(n, carry):
        place = target_of(n, 1)

        @pl.when(inside(place) & (n != 13))
        def _():
            pl.semaphore_signal(barrier, inc=1, device_id=place, device_id_type=MESH)

        return carry

    lax.fori_loop(0, 27, greet, 0)

    codes = cell[...]
    code_a, rest = split_by(codes, cy * cz)
    code_b, code_c = split_by(rest, cz)
    tiles = tile[...]
    tile_a, rest = split_by(tiles, nb * nc)
    tile_b, tile_c = split_by(rest, nc)
    neighbour[...] = ((tile_a - a + 1) * 3 + tile_b - b + 1) * 3 + tile_c - c + 1
    vals[...] = jnp.zeros_like(vals)
    for r in range(run_count):
        span = slice(r * cap, (r + 1) * cap)
        vals[r, 0:3, :] = force[:, span]
        for d, code in enumerate((code_a, code_b, code_c)):
            vals[r, 3 + d : 4 + d, :] = code[r : r + 1].astype(jnp.float32) + offset[d : d + 1, span]

    pl.semaphore_wait(
        barrier,
        (1 + (a > 0).astype(jnp.int32) + (a < na - 1).astype(jnp.int32))
        * (1 + (b > 0).astype(jnp.int32) + (b < nb - 1).astype(jnp.int32))
        * (1 + (c > 0).astype(jnp.int32) + (c < nc - 1).astype(jnp.int32))
        - 1,
    )

    def pay_copy(n, place):
        return pltpu.make_async_remote_copy(
            pay.at[n], slots.at[n], pay_ss.at[n], pay_rs.at[n], device_id=place, device_id_type=MESH
        )

    def send_points(n, carry):
        block = jnp.zeros(vals.shape[1:], jnp.float32)
        for r in range(run_count):
            block = jnp.where(neighbour[r : r + 1, :] == n, vals[r], block)
        pay[n] = block
        place = target_of(n, 1)

        @pl.when(inside(place) & (n != 13))
        def _():
            pay_copy(n, place).start()

        return carry

    lax.fori_loop(0, 27, send_points, 0)
    slots[13] = pay[13]

    lane = lax.broadcasted_iota(jnp.int32, (cy, cz), 1)

    def pack_plane(s, h, g, t, v):
        within = 4 * g + t
        for comp in range(3):
            y_send[s, 0, h, comp, g, 2 * t : 2 * t + 2, :] = v[comp][0:2]
            y_send[s, 1, h, comp, g, 2 * t : 2 * t + 2, :] = v[comp][cy - 2 : cy]
            moved = pltpu.roll(v[comp], 4 * within + 2, 1)
            z_send[s, h, comp] = jnp.where((lane >> 2) == within, moved, z_send[s, h, comp])

    def beside(dim, side):
        step = 2 * side - 1
        place = tuple(p + step if d == dim else p for d, p in enumerate(where_am_i))
        ok = place[dim] >= 0 if side == 0 else place[dim] < counts[dim]
        return place, ok

    def x_copy(s, side, place):
        source, target = (2, cx + 2) if side == 0 else (cx, 0)
        rows = slice(8, 8 + cy)
        return pltpu.make_async_remote_copy(
            field.at[s, :, pl.ds(source, 2), rows],
            field.at[s, :, pl.ds(target, 2), rows],
            x_ss.at[s, side],
            x_rs.at[s, side],
            device_id=place,
            device_id_type=MESH,
        )

    def y_copy(s, side, h, place):
        return pltpu.make_async_remote_copy(
            y_send.at[s, side, h],
            y_recv.at[s, side, h],
            y_ss.at[s, side, h],
            y_rs.at[s, side, h],
            device_id=place,
            device_id_type=MESH,
        )

    def z_copy(s, side, h, place):
        return pltpu.make_async_remote_copy(
            z_send.at[s, h],
            z_recv.at[s, side, h],
            z_ss.at[s, side, h],
            z_rs.at[s, side, h],
            device_id=place,
            device_id_type=MESH,
        )

    def send_half(s, h):
        for side in (0, 1):
            place, ok = beside(1, side)
            pl.when(ok)(lambda: y_copy(s, side, h, place).start())
        for side in (0, 1):
            place, ok = beside(2, side)
            pl.when(ok)(lambda: z_copy(s, side, h, place).start())
            place, ok = beside(0, side)
            pl.when(ok & (h == side))(lambda: x_copy(s, side, place).start())

    def wait_half(s, h):
        for side in (0, 1):
            place, ok = beside(0, 1 - side)
            pl.when(ok & (h == 1 - side))(lambda: x_copy(s, side, place).wait_recv())
            place, ok = beside(2, 1 - side)
            pl.when(ok)(lambda: z_copy(s, side, h, place).wait_recv())
            place, ok = beside(1, 1 - side)
            pl.when(ok)(lambda: y_copy(s, side, h, place).wait_recv())

    def wait_sends(s):
        for side in (0, 1):
            place, ok = beside(0, side)
            pl.when(ok)(lambda: x_copy(s, side, place).wait_send())
            for h in (0, 1):
                place, ok = beside(1, side)
                pl.when(ok)(lambda: y_copy(s, side, h, place).wait_send())
                place, ok = beside(2, side)
                pl.when(ok)(lambda: z_copy(s, side, h, place).wait_send())

    first = lax.rem(a, 2)
    z_send[...] = jnp.zeros_like(z_send)

    for turn in range(2):
        h = first if turn == 0 else 1 - first

        def stage_in(g, carry):
            for t in range(4):
                i = h * half_planes + 4 * g + t
                v = [vel[comp, i] for comp in range(3)]
                for comp in range(3):
                    field[0, comp, i + 2, 8 : 8 + cy, :] = v[comp]
                pack_plane(0, h, g, t, v)
            return carry

        lax.fori_loop(0, groups, stage_in, 0)
        send_half(0, h)

    def span_of(p, count):
        low = jnp.where(p < count - 1, 0, 1)
        high = jnp.where(p > 0, 2, 1)
        return low, high - low + 1

    (low_a, in_a), (low_b, in_b), (low_c, in_c) = (
        span_of(p, count) for p, count in zip(where_am_i, counts)
    )
    blocks = in_a * in_b * in_c
    pairs = (blocks + 1) // 2

    def block_of(v):
        n = (low_a + v // (in_b * in_c)) * 9 + (low_b + v // in_c % in_b) * 3 + low_c + v % in_c
        return jnp.where(v < blocks, n, 27)

    def wait_points(n, carry):
        place = target_of(n, -1)

        @pl.when(inside(place) & (n != 13))
        def _():
            pay_copy(n, place).wait_recv()

        return carry

    lax.fori_loop(0, 27, wait_points, 0)

    def pair_slots(pair):
        n0, n1 = block_of(2 * pair), block_of(2 * pair + 1)
        return n0, n1, jnp.concatenate([slots[n0], slots[n1]], axis=1)

    force_acc[...] = jnp.zeros_like(force_acc)

    def spread(pair, carry):
        _, _, s = pair_slots(pair)
        wx = weights(s[3:4], cx)
        wy = weights(s[4:5], cy)
        wz = weights(s[5:6], cz)
        a_high, a_low = halves(jnp.concatenate([s[d : d + 1] * wx for d in range(3)], axis=0))
        for j in range(cy):
            high, low = halves(wy[j : j + 1] * wz)
            w_high[j * cz : (j + 1) * cz, :] = high
            w_low[j * cz : (j + 1) * cz, :] = low
        right = jnp.concatenate([a_high, a_low, a_high], axis=1)
        left = jnp.concatenate([w_high[...], w_high[...], w_low[...]], axis=1)
        force_acc[...] += lax.dot_general(
            left, right, (((1,), (1,)), ((), ())), preferred_element_type=jnp.float32
        )
        return carry

    lax.fori_loop(0, pairs, spread, 0)

    for j in range(cy):
        turned = force_acc[j * cz : (j + 1) * cz, :].T
        for comp in range(3):
            forcing[pl.ds(comp * cx * cy + j, cx, stride=cy), :] = turned[comp * cx : (comp + 1) * cx]

    for s in range(3):
        for turn in range(2):
            h = first if turn == 0 else 1 - first
            wait_half(s, h)
            for comp in range(3):
                z_mix[comp] = jnp.where((lane & 3) < 2, z_recv[s, 1, h, comp], z_recv[s, 0, h, comp])

            def advance(g, carry):
                for t in range(4):
                    i = h * half_planes + 4 * g + t
                    centre = [field[s, comp, i + 2, 8 : 8 + cy, :] for comp in range(3)]
                    nu = visc[i]
                    result = []
                    for comp in range(3):
                        v = centre[comp]
                        field[s, comp, i + 2, 6:8, :] = y_recv[s, 1, h, comp, g, 2 * t : 2 * t + 2, :]
                        field[s, comp, i + 2, 8 + cy : 10 + cy, :] = y_recv[
                            s, 0, h, comp, g, 2 * t : 2 * t + 2, :
                        ]
                        ends = pltpu.roll(z_mix[comp], cz - 2 - 4 * (4 * g + t), 1)
                        around = (
                            [field[s, comp, i + 2 + m, 8 : 8 + cy, :] for m in (-2, -1, 1, 2)],
                            [field[s, comp, i + 2, 8 + m : 8 + m + cy, :] for m in (-2, -1, 1, 2)],
                            [
                                pltpu.roll(jnp.where(lane >= cz - 2, ends, v), 2, 1),
                                pltpu.roll(jnp.where(lane >= cz - 1, ends, v), 1, 1),
                                pltpu.roll(jnp.where(lane < 1, ends, v), cz - 1, 1),
                                pltpu.roll(jnp.where(lane < 2, ends, v), cz - 2, 1),
                            ],
                        )
                        spreading = -6.0 * v
                        carried = jnp.zeros_like(v)
                        for d in range(3):
                            m2, m1, p1, p2 = around[d]
                            carried += centre[d] * (8.0 * (p1 - m1) - (p2 - m2))
                            spreading += p1 + m1
                        row = pl.multiple_of((comp * cx + i) * cy, cy)
                        tend = nu * spreading - carried * (1.0 / 12.0) + forcing[pl.ds(row, cy), :]
                        moved = v + time_step * tend
                        if s == 1:
                            moved = 0.75 * vel[comp, i] + 0.25 * moved
                        elif s == 2:
                            moved = one_third * vel[comp, i] + two_thirds * moved
                        result.append(moved)
                        if s < 2:
                            field[s + 1, comp, i + 2, 8 : 8 + cy, :] = moved
                        else:
                            out_vel[comp, i] = moved
                            high, low = halves(moved)
                            v_split[pl.ds(row, cy), 0:cz] = high
                            v_split[pl.ds(row, cy), cz : 2 * cz] = low
                    if s < 2:
                        pack_plane(s + 1, h, g, t, result)
                return carry

            lax.fori_loop(0, groups, advance, 0)
            if s < 2:
                send_half(s + 1, h)

    def ret_copy(n, place):
        return pltpu.make_async_remote_copy(
            sampled.at[n],
            returned.at[n],
            ret_ss.at[n],
            ret_rs.at[n],
            device_id=place,
            device_id_type=MESH,
        )

    sampled[...] = jnp.zeros_like(sampled)

    def sample(pair, carry):
        n0, n1, s = pair_slots(pair)
        wx = weights(s[3:4], cx)
        wy = weights(s[4:5], cy)
        high, low = halves(weights(s[5:6], cz))
        right = jnp.concatenate([high, high, low, low], axis=0)
        for comp in range(3):
            v = v_split[comp * cx * cy : (comp + 1) * cx * cy, :]
            product[...] = jnp.dot(
                jnp.concatenate([v, v], axis=1), right, preferred_element_type=jnp.float32
            )
            total = jnp.zeros((cy, 2 * cap), jnp.float32)
            for i in range(cx):
                total += wx[i : i + 1] * product[i * cy : (i + 1) * cy, :]
            row = jnp.sum(total * wy, axis=0, keepdims=True)
            sampled[n0, comp : comp + 1, :] = row[:, :cap]
            sampled[n1, comp : comp + 1, :] = row[:, cap:]
        for n in (n0, n1):

            @pl.when((n != 13) & (n < 27))
            def _():
                ret_copy(n, target_of(n, -1)).start()

        return carry

    lax.fori_loop(0, pairs, sample, 0)
    returned[13] = sampled[13]

    def wait_returned(n, carry):
        @pl.when(inside(target_of(n, 1)) & (n != 13))
        def _():
            ret_copy(n, target_of(n, 1)).wait_recv()

        return carry

    lax.fori_loop(0, 27, wait_returned, 0)
    for r in range(run_count):

        def pick(n, block):
            return jnp.where(neighbour[r : r + 1, :] == n, returned[n], block)

        block = lax.fori_loop(0, 27, pick, jnp.zeros(returned.shape[1:], jnp.float32), unroll=True)
        out_pts[:, r * cap : (r + 1) * cap] = block[0:3]

    def finish(n, carry):
        @pl.when(inside(target_of(n, 1)) & (n != 13))
        def _():
            pay_copy(n, target_of(n, 1)).wait_send()

        @pl.when(inside(target_of(n, -1)) & (n != 13))
        def _():
            ret_copy(n, target_of(n, -1)).wait_send()

        return carry

    lax.fori_loop(0, 27, finish, 0)
    for s in range(3):
        wait_sends(s)


def per_device(velocity, viscosity, point_force, point_offset, point_cell, point_tile):
    _, cx, cy, cz = velocity.shape
    points = point_force.shape[1]
    cap = points // run_count
    mesh_sizes = tuple(lax.axis_size(axis) for axis in ("gx", "gy", "gz"))
    sizes = (mesh_sizes, (cx, cy, cz), cap)
    half, groups = cx // 2, cx // 8
    f32, bf16 = jnp.float32, jnp.bfloat16
    dma = pltpu.SemaphoreType.DMA
    whole = pl.BlockSpec(memory_space=pltpu.VMEM)
    return pl.pallas_call(
        functools.partial(kernel, sizes),
        out_shape=(
            jax.ShapeDtypeStruct(velocity.shape, f32),
            jax.ShapeDtypeStruct(point_force.shape, f32),
        ),
        in_specs=[whole] * 6,
        out_specs=(whole, whole),
        scratch_shapes=[
            pltpu.VMEM((3, 3, cx + 4, cy + 16, cz), f32),
            pltpu.VMEM((cy * cz, 3 * cx), f32),
            pltpu.VMEM((3 * cx * cy, cz), f32),
            pltpu.VMEM((cy * cz, 2 * cap), bf16),
            pltpu.VMEM((cy * cz, 2 * cap), bf16),
            pltpu.VMEM((cx * cy, 2 * cap), f32),
            pltpu.VMEM((3 * cx * cy, 2 * cz), bf16),
            pltpu.VMEM((run_count, 8, cap), f32),
            pltpu.VMEM((run_count, cap), jnp.int32),
            pltpu.VMEM((27, 8, cap), f32),
            pltpu.VMEM((28, 8, cap), f32),
            pltpu.VMEM((28, 8, cap), f32),
            pltpu.VMEM((27, 8, cap), f32),
            pltpu.VMEM((3, 2, 2, 3, groups, 8, cz), f32),
            pltpu.VMEM((3, 2, 2, 3, groups, 8, cz), f32),
            pltpu.VMEM((3, 2, 3, cy, cz), f32),
            pltpu.VMEM((3, 2, 2, 3, cy, cz), f32),
            pltpu.VMEM((3, cy, cz), f32),
            dma((27,)),
            dma((27,)),
            dma((27,)),
            dma((27,)),
            dma((3, 2)),
            dma((3, 2)),
            dma((3, 2, 2)),
            dma((3, 2, 2)),
            dma((3, 2, 2)),
            dma((3, 2, 2)),
        ],
        compiler_params=pltpu.CompilerParams(
            collective_id=0, has_side_effects=True, vmem_limit_bytes=56 * 2**20
        ),
        name="farm_step",
    )(
        velocity,
        viscosity,
        point_force,
        point_offset,
        point_cell.reshape(run_count, cap),
        point_tile.reshape(run_count, cap),
    )


def solution(mesh):
    in_specs = (
        P(None, "gx", "gy", "gz"),
        P("gx", "gy", "gz"),
        P(None, ("gx", "gy", "gz")),
        P(None, ("gx", "gy", "gz")),
        P(("gx", "gy", "gz")),
        P(("gx", "gy", "gz"), None),
    )
    out_specs = (P(None, "gx", "gy", "gz"), P(None, ("gx", "gy", "gz")))
    return jax.shard_map(
        per_device, mesh=mesh, in_specs=in_specs, out_specs=out_specs, check_vma=False
    )
```

profile of v0, /device:TPU:0, one launch (start us, length us, event | category | flops | bytes accessed | tf_op | source)
XLA Modules:
  0.0 67.0 jit_solution(3845814287612172302)
XLA Ops:
  0.6 63.1 %farm_step.1 = (f32[3,64,16,128]{3,2,1,0:T(8,128)}, f32[3,1024]{1,0:T(4,128)}) custom-call(f32[3,64,16,128]{3,2,1,0:T(8,128)} %vel.1, f32[64,16,128]{2,1,0:T(8,128)} %visc.1, f32[3,1024]{1,0:T(4,128)} %force.1, f32[3,1024]{1,0:T(4,128)} %offset.1, s32[8,128]{1,0:T(8,128)} %bitcast.2, s32[8,128]{1,0:T(8,128)} %bitcast.3), custom_call_target="tpu_custom_call" | custom-call | tf_op jit(solution)/shard_map/farm_step/pallas_call | solution.py:453
  63.7 0.0 copy-start
  63.7 2.7 %copy.10 = f32[3,64,16,128]{3,2,1,0:T(8,128)} copy(f32[3,64,16,128]{3,2,1,0:T(8,128)} %get-tuple-element.4) | data formatting | bytes 3145728
  66.4 0.0 copy-done
  66.4 0.6 copy.11
Async XLA Ops:
  63.7 2.7 %copy-start = (f32[3,1024]{1,0:T(4,128)S(1)}, f32[3,1024]{1,0:T(4,128)}, u32[]{:S(2)}) copy-start(f32[3,1024]{1,0:T(4,128)} %get-tuple-element.5) | copy-start | bytes 36868
where the time goes:
time: 67.2 us; the launch traced here: 67 us
  Pallas kernels  63.1 us (94%)
  local copies, waits for them, and re-layouts  3.27 us (5%)
    pallas_call x1, Pallas kernels, per_device(): pl.pallas_call(functools.partial(kernel, sizes), out_shape=(jax.ShapeDtyp...  63.1 us
    unnamed x4, local copies, waits for them, and re-layouts  3.27 us

commit v1 on v0

v1 whole, which is shorter than its diff:
```python
import functools

import jax
import jax.numpy as jnp
from jax import lax
from jax.experimental import pallas as pl
from jax.experimental.pallas import tpu as pltpu
from jax.sharding import PartitionSpec as P

MESH = pl.DeviceIdType.MESH
time_step = 0.1
kernel_width = 2.0
one_third = 1.0 / 3.0
two_thirds = 2.0 / 3.0
run_count = 8


def split_by(x, n):
    if n & (n - 1) == 0:
        bits = n.bit_length() - 1
        return lax.shift_right_logical(x, jnp.int32(bits)), x & (n - 1)
    return lax.div(x, jnp.int32(n)), lax.rem(x, jnp.int32(n))


def halves(x):
    high = x.astype(jnp.bfloat16)
    low = (x - high.astype(jnp.float32)).astype(jnp.bfloat16)
    return high, low


def weights(centre, cells):
    middles = lax.broadcasted_iota(jnp.int32, (cells, centre.shape[1]), 0).astype(jnp.float32) + 0.5
    scaled = (middles - centre) / kernel_width
    unscaled = jnp.exp(-scaled * scaled)
    return unscaled / jnp.sum(unscaled, axis=0, keepdims=True)


def kernel(
    sizes,
    vel,
    visc_in,
    force,
    offset,
    cell,
    tile,
    out_vel,
    out_pts,
    field,
    visc,
    fresh,
    local_sem,
    force_acc,
    forcing,
    w_high,
    w_low,
    product,
    v_split,
    vals,
    neighbour,
    pay,
    slots,
    sampled,
    returned,
    y_send,
    y_recv,
    z_send,
    z_recv,
    z_mix,
    pay_ss,
    pay_rs,
    ret_ss,
    ret_rs,
    x_ss,
    x_rs,
    y_ss,
    y_rs,
    z_ss,
    z_rs,
):
    (na, nb, nc), (cx, cy, cz), cap = sizes
    a, b, c = (lax.axis_index(axis) for axis in ("gx", "gy", "gz"))
    where_am_i = (a, b, c)
    counts = (na, nb, nc)
    rows = cy // 2
    pack_groups = cz // 16
    packs = cx // (cz // 4)

    def step_of(n):
        return n // 9 - 1, n // 3 % 3 - 1, n % 3 - 1

    def inside(place):
        ok = (place[0] >= 0) & (place[0] < na)
        ok &= (place[1] >= 0) & (place[1] < nb)
        return ok & (place[2] >= 0) & (place[2] < nc)

    def target_of(n, sign):
        da, db, dc = step_of(n)
        return a + sign * da, b + sign * db, c + sign * dc

    vel_copy = pltpu.make_async_copy(
        vel, field.at[0, :, pl.ds(2, cx), pl.ds(8, cy)], local_sem.at[0]
    )
    vel_copy.start()
    visc_copy = pltpu.make_async_copy(visc_in, visc, local_sem.at[1])
    visc_copy.start()

    slots[...] = jnp.zeros_like(slots)
    returned[...] = jnp.zeros_like(returned)
    y_recv[...] = jnp.zeros_like(y_recv)
    z_recv[...] = jnp.zeros_like(z_recv)
    edge = jnp.zeros((3, 2) + field.shape[3:], jnp.float32)
    for s in range(3):
        field[s, :, 0:2] = edge
        field[s, :, cx + 2 : cx + 4] = edge

    barrier = pltpu.get_barrier_semaphore()

    def greet(n, carry):
        place = target_of(n, 1)

        @pl.when(inside(place) & (n != 13))
        def _():
            pl.semaphore_signal(barrier, inc=1, device_id=place, device_id_type=MESH)

        return carry

    lax.fori_loop(0, 27, greet, 0)

    codes = cell[...]
    code_a, rest = split_by(codes, cy * cz)
    code_b, code_c = split_by(rest, cz)
    tiles = tile[...]
    tile_a, rest = split_by(tiles, nb * nc)
    tile_b, tile_c = split_by(rest, nc)
    neighbour[...] = ((tile_a - a + 1) * 3 + tile_b - b + 1) * 3 + tile_c - c + 1
    vals[...] = jnp.zeros_like(vals)
    for r in range(run_count):
        span = slice(r * cap, (r + 1) * cap)
        vals[r, 0:3, :] = force[:, span]
        for d, code in enumerate((code_a, code_b, code_c)):
            vals[r, 3 + d : 4 + d, :] = code[r : r + 1].astype(jnp.float32) + offset[d : d + 1, span]

    pl.semaphore_wait(
        barrier,
        (1 + (a > 0).astype(jnp.int32) + (a < na - 1).astype(jnp.int32))
        * (1 + (b > 0).astype(jnp.int32) + (b < nb - 1).astype(jnp.int32))
        * (1 + (c > 0).astype(jnp.int32) + (c < nc - 1).astype(jnp.int32))
        - 1,
    )

    def pay_copy(n, place):
        return pltpu.make_async_remote_copy(
            pay.at[n], slots.at[n], pay_ss.at[n], pay_rs.at[n], device_id=place, device_id_type=MESH
        )

    def send_points(n, carry):
        block = jnp.zeros(vals.shape[1:], jnp.float32)
        for r in range(run_count):
            block = jnp.where(neighbour[r : r + 1, :] == n, vals[r], block)
        pay[n] = block
        place = target_of(n, 1)

        @pl.when(inside(place) & (n != 13))
        def _():
            pay_copy(n, place).start()

        return carry

    lax.fori_loop(0, 27, send_points, 0)
    slots[13] = pay[13]

    lane = lax.broadcasted_iota(jnp.int32, (rows, cz), 1)

    def pack_planes(s, h, g, planes):
        inner = slice(0, 2) if h == 0 else slice(rows - 2, rows)
        pack, place = g // pack_groups, g % pack_groups
        for comp in range(3):
            packed = z_send[s, h, comp, pack]
            for t in range(4):
                v = planes[t][comp]
                y_send[s, h, comp, g, 2 * t : 2 * t + 2, :] = v[inner]
                within = 4 * place + t
                packed = jnp.where((lane >> 2) == within, pltpu.roll(v, 4 * within + 2, 1), packed)
            z_send[s, h, comp, pack] = packed

    def beside(dim, side):
        step = 2 * side - 1
        place = tuple(p + step if d == dim else p for d, p in enumerate(where_am_i))
        ok = place[dim] >= 0 if side == 0 else place[dim] < counts[dim]
        return place, ok

    def x_copy(s, side, h, place):
        source, target = (2, cx + 2) if side == 0 else (cx, 0)
        span = slice(8 + rows * h, 8 + rows * (h + 1))
        return pltpu.make_async_remote_copy(
            field.at[s, :, pl.ds(source, 2), span],
            field.at[s, :, pl.ds(target, 2), span],
            x_ss.at[s, side, h],
            x_rs.at[s, side, h],
            device_id=place,
            device_id_type=MESH,
        )

    def y_copy(s, side, place):
        return pltpu.make_async_remote_copy(
            y_send.at[s, side],
            y_recv.at[s, side],
            y_ss.at[s, side],
            y_rs.at[s, side],
            device_id=place,
            device_id_type=MESH,
        )

    def z_copy(s, side, h, place):
        return pltpu.make_async_remote_copy(
            z_send.at[s, h],
            z_recv.at[s, side, h],
            z_ss.at[s, side, h],
            z_rs.at[s, side, h],
            device_id=place,
            device_id_type=MESH,
        )

    def send_half(s, h):
        place, ok = beside(1, h)
        pl.when(ok)(lambda: y_copy(s, h, place).start())
        for side in (0, 1):
            z_place, z_ok = beside(2, side)
            pl.when(z_ok)(lambda: z_copy(s, side, h, z_place).start())
            x_place, x_ok = beside(0, side)
            pl.when(x_ok)(lambda: x_copy(s, side, h, x_place).start())

    def wait_half(s, h):
        for side in (0, 1):
            x_place, x_ok = beside(0, 1 - side)
            pl.when(x_ok)(lambda: x_copy(s, side, h, x_place).wait_recv())
            z_place, z_ok = beside(2, 1 - side)
            pl.when(z_ok)(lambda: z_copy(s, side, h, z_place).wait_recv())
        place, ok = beside(1, h)
        pl.when(ok)(lambda: y_copy(s, 1 - h, place).wait_recv())

    def wait_sends(s):
        for side in (0, 1):
            y_place, y_ok = beside(1, side)
            pl.when(y_ok)(lambda: y_copy(s, side, y_place).wait_send())
            x_place, x_ok = beside(0, side)
            z_place, z_ok = beside(2, side)
            for h in (0, 1):
                pl.when(x_ok)(lambda: x_copy(s, side, h, x_place).wait_send())
                pl.when(z_ok)(lambda: z_copy(s, side, h, z_place).wait_send())

    first = lax.rem(b, 2)

    def by_turn(turn, work):
        pl.when(first == turn)(lambda: work(0))
        pl.when(first != turn)(lambda: work(1))

    def half_of(turn):
        return first if turn == 0 else 1 - first

    z_send[...] = jnp.zeros_like(z_send)
    vel_copy.wait()

    def first_faces(h):
        def one(g, carry):
            span = slice(8 + rows * h, 8 + rows * (h + 1))
            pack_planes(
                0, h, g, [[field[0, comp, 4 * g + t + 2, span, :] for comp in range(3)] for t in range(4)]
            )
            return carry

        lax.fori_loop(0, cx // 4, one, 0)
        send_half(0, h)

    for turn in range(2):
        by_turn(turn, first_faces)

    def span_of(p, count):
        low = jnp.where(p < count - 1, 0, 1)
        high = jnp.where(p > 0, 2, 1)
        return low, high - low + 1

    (low_a, in_a), (low_b, in_b), (low_c, in_c) = (
        span_of(p, count) for p, count in zip(where_am_i, counts)
    )
    blocks = in_a * in_b * in_c
    pairs = (blocks + 1) // 2

    def block_of(v):
        n = (low_a + v // (in_b * in_c)) * 9 + (low_b + v // in_c % in_b) * 3 + low_c + v % in_c
        return jnp.where(v < blocks, n, 27)

    def wait_points(n, carry):
        place = target_of(n, -1)

        @pl.when(inside(place) & (n != 13))
        def _():
            pay_copy(n, place).wait_recv()

        return carry

    lax.fori_loop(0, 27, wait_points, 0)

    def pair_slots(pair):
        n0, n1 = block_of(2 * pair), block_of(2 * pair + 1)
        return n0, n1, jnp.concatenate([slots[n0], slots[n1]], axis=1)

    force_acc[...] = jnp.zeros_like(force_acc)
    visc_copy.wait()

    def half_rows(w, h):
        return jnp.where(h == 0, w[:rows], w[rows:])

    def spread_half(turn):
        h = half_of(turn)

        def spread(pair, carry):
            _, _, s = pair_slots(pair)
            wx = weights(s[3:4], cx)
            wy = half_rows(weights(s[4:5], cy), h)
            wz = weights(s[5:6], cz)
            a_high, a_low = halves(jnp.concatenate([s[d : d + 1] * wx for d in range(3)], axis=0))
            for j in range(rows):
                high, low = halves(wy[j : j + 1] * wz)
                w_high[j * cz : (j + 1) * cz, :] = high
                w_low[j * cz : (j + 1) * cz, :] = low
            right = jnp.concatenate([a_high, a_low, a_high], axis=1)
            left = jnp.concatenate([w_high[...], w_high[...], w_low[...]], axis=1)
            force_acc[turn] += lax.dot_general(
                left, right, (((1,), (1,)), ((), ())), preferred_element_type=jnp.float32
            )
            return carry

        lax.fori_loop(0, pairs, spread, 0)
        for j in range(rows):
            turned = force_acc[turn, j * cz : (j + 1) * cz, :].T
            for comp in range(3):
                forcing[turn, pl.ds(comp * cx * rows + j, cx, stride=rows), :] = turned[
                    comp * cx : (comp + 1) * cx
                ]

    def advance_half(s, turn, h):
        wait_half(s, h)
        for comp in range(3):
            for pack in range(packs):
                z_mix[comp, pack] = jnp.where(
                    (lane & 3) < 2, z_recv[s, 1, h, comp, pack], z_recv[s, 0, h, comp, pack]
                )
        low = 8 + rows * h
        span = slice(low, low + rows)
        halo = slice(6, 8) if h == 0 else slice(8 + cy, 10 + cy)

        def advance(g, carry):
            pack, place = g // pack_groups, g % pack_groups
            planes = []
            for t in range(4):
                i = 4 * g + t
                centre = [field[s, comp, i + 2, span, :] for comp in range(3)]
                nu = visc[i, rows * h : rows * (h + 1), :]
                result = []
                for comp in range(3):
                    v = centre[comp]
                    field[s, comp, i + 2, halo, :] = y_recv[s, 1 - h, comp, g, 2 * t : 2 * t + 2, :]
                    ends = pltpu.roll(z_mix[comp, pack], cz - 2 - 4 * (4 * place + t), 1)
                    around = (
                        [field[s, comp, i + 2 + m, span, :] for m in (-2, -1, 1, 2)],
                        [field[s, comp, i + 2, low + m : low + m + rows, :] for m in (-2, -1, 1, 2)],
                        [
                            pltpu.roll(jnp.where(lane >= cz - 2, ends, v), 2, 1),
                            pltpu.roll(jnp.where(lane >= cz - 1, ends, v), 1, 1),
                            pltpu.roll(jnp.where(lane < 1, ends, v), cz - 1, 1),
                            pltpu.roll(jnp.where(lane < 2, ends, v), cz - 2, 1),
                        ],
                    )
                    spreading = -6.0 * v
                    carried = jnp.zeros_like(v)
                    for d in range(3):
                        m2, m1, p1, p2 = around[d]
                        carried += centre[d] * (8.0 * (p1 - m1) - (p2 - m2))
                        spreading += p1 + m1
                    row = pl.multiple_of((comp * cx + i) * rows, rows)
                    tend = nu * spreading - carried * (1.0 / 12.0) + forcing[turn, pl.ds(row, rows), :]
                    moved = v + time_step * tend
                    if s == 1:
                        moved = 0.75 * field[0, comp, i + 2, span, :] + 0.25 * moved
                    elif s == 2:
                        moved = one_third * field[0, comp, i + 2, span, :] + two_thirds * moved
                    result.append(moved)
                    if s < 2:
                        field[s + 1, comp, i + 2, span, :] = moved
                    else:
                        fresh[comp, i, rows * h : rows * (h + 1), :] = moved
                planes.append(result)
            if s < 2:
                pack_planes(s + 1, h, g, planes)
            else:
                for comp in range(3):
                    for t in (0, 2):
                        row = pl.multiple_of((comp * cx + 4 * g + t) * rows, 2 * rows)
                        high, low_part = halves(
                            jnp.concatenate([planes[t][comp], planes[t + 1][comp]], axis=0)
                        )
                        v_split[turn, pl.ds(row, 2 * rows), 0:cz] = high
                        v_split[turn, pl.ds(row, 2 * rows), cz : 2 * cz] = low_part
            return carry

        lax.fori_loop(0, cx // 4, advance, 0)
        if s < 2:
            send_half(s + 1, h)
        else:
            out_copy(h).start()

    def out_copy(h):
        span = slice(rows * h, rows * (h + 1))
        return pltpu.make_async_copy(fresh.at[:, :, span], out_vel.at[:, :, span], local_sem.at[2 + h])

    def section(s, turn):
        by_turn(turn, lambda h: advance_half(s, turn, h))

    spread_half(0)
    section(0, 0)
    spread_half(1)
    section(0, 1)
    section(1, 0)
    section(1, 1)
    section(2, 0)

    def ret_copy(n, place):
        return pltpu.make_async_remote_copy(
            sampled.at[n],
            returned.at[n],
            ret_ss.at[n],
            ret_rs.at[n],
            device_id=place,
            device_id_type=MESH,
        )

    sampled[...] = jnp.zeros_like(sampled)

    def sample_half(turn):
        h = half_of(turn)

        def sample(pair, carry):
            n0, n1, s = pair_slots(pair)
            wx = weights(s[3:4], cx)
            wy = half_rows(weights(s[4:5], cy), h)
            high, low = halves(weights(s[5:6], cz))
            right = jnp.concatenate([high, high, low, low], axis=0)
            for comp in range(3):
                v = v_split[turn, comp * cx * rows : (comp + 1) * cx * rows, :]
                product[comp] = jnp.dot(
                    jnp.concatenate([v, v], axis=1), right, preferred_element_type=jnp.float32
                )
            for comp in range(3):
                total = jnp.zeros((rows, 2 * cap), jnp.float32)
                for i in range(cx):
                    total += wx[i : i + 1] * product[comp, i * rows : (i + 1) * rows, :]
                row = jnp.sum(total * wy, axis=0, keepdims=True)
                sampled[n0, comp : comp + 1, :] += row[:, :cap]
                sampled[n1, comp : comp + 1, :] += row[:, cap:]
            if turn == 1:
                for n in (n0, n1):

                    @pl.when((n != 13) & (n < 27))
                    def _():
                        ret_copy(n, target_of(n, -1)).start()

            return carry

        lax.fori_loop(0, pairs, sample, 0)

    sample_half(0)
    section(2, 1)
    sample_half(1)
    returned[13] = sampled[13]

    def wait_returned(n, carry):
        @pl.when(inside(target_of(n, 1)) & (n != 13))
        def _():
            ret_copy(n, target_of(n, 1)).wait_recv()

        return carry

    lax.fori_loop(0, 27, wait_returned, 0)
    for r in range(run_count):

        def pick(n, block):
            return jnp.where(neighbour[r : r + 1, :] == n, returned[n], block)

        block = lax.fori_loop(0, 27, pick, jnp.zeros(returned.shape[1:], jnp.float32), unroll=True)
        out_pts[:, r * cap : (r + 1) * cap] = block[0:3]

    def finish(n, carry):
        @pl.when(inside(target_of(n, 1)) & (n != 13))
        def _():
            pay_copy(n, target_of(n, 1)).wait_send()

        @pl.when(inside(target_of(n, -1)) & (n != 13))
        def _():
            ret_copy(n, target_of(n, -1)).wait_send()

        return carry

    lax.fori_loop(0, 27, finish, 0)
    for s in range(3):
        wait_sends(s)
    for h in range(2):
        out_copy(h).wait()


def per_device(velocity, viscosity, point_force, point_offset, point_cell, point_tile):
    _, cx, cy, cz = velocity.shape
    points = point_force.shape[1]
    cap = points // run_count
    mesh_sizes = tuple(lax.axis_size(axis) for axis in ("gx", "gy", "gz"))
    sizes = (mesh_sizes, (cx, cy, cz), cap)
    rows, groups, packs = cy // 2, cx // 4, cx // (cz // 4)
    f32, bf16 = jnp.float32, jnp.bfloat16
    dma = pltpu.SemaphoreType.DMA
    whole = pl.BlockSpec(memory_space=pltpu.VMEM)
    anywhere = pl.BlockSpec(memory_space=pl.ANY)
    return pl.pallas_call(
        functools.partial(kernel, sizes),
        out_shape=(
            jax.ShapeDtypeStruct(velocity.shape, f32),
            jax.ShapeDtypeStruct(point_force.shape, f32),
        ),
        in_specs=[anywhere] * 2 + [whole] * 4,
        out_specs=(anywhere, whole),
        scratch_shapes=[
            pltpu.VMEM((3, 3, cx + 4, cy + 16, cz), f32),
            pltpu.VMEM((cx, cy, cz), f32),
            pltpu.VMEM((3, cx, cy, cz), f32),
            dma((4,)),
            pltpu.VMEM((2, rows * cz, 3 * cx), f32),
            pltpu.VMEM((2, 3 * cx * rows, cz), f32),
            pltpu.VMEM((rows * cz, 2 * cap), bf16),
            pltpu.VMEM((rows * cz, 2 * cap), bf16),
            pltpu.VMEM((3, cx * rows, 2 * cap), f32),
            pltpu.VMEM((2, 3 * cx * rows, 2 * cz), bf16),
            pltpu.VMEM((run_count, 8, cap), f32),
            pltpu.VMEM((run_count, cap), jnp.int32),
            pltpu.VMEM((27, 8, cap), f32),
            pltpu.VMEM((28, 8, cap), f32),
            pltpu.VMEM((28, 8, cap), f32),
            pltpu.VMEM((27, 8, cap), f32),
            pltpu.VMEM((3, 2, 3, groups, 8, cz), f32),
            pltpu.VMEM((3, 2, 3, groups, 8, cz), f32),
            pltpu.VMEM((3, 2, 3, packs, rows, cz), f32),
            pltpu.VMEM((3, 2, 2, 3, packs, rows, cz), f32),
            pltpu.VMEM((3, packs, rows, cz), f32),
            dma((27,)),
            dma((27,)),
            dma((27,)),
            dma((27,)),
            dma((3, 2, 2)),
            dma((3, 2, 2)),
            dma((3, 2)),
            dma((3, 2)),
            dma((3, 2, 2)),
            dma((3, 2, 2)),
        ],
        compiler_params=pltpu.CompilerParams(
            collective_id=0, has_side_effects=True, vmem_limit_bytes=56 * 2**20
        ),
        name="farm_step",
    )(
        velocity,
        viscosity,
        point_force,
        point_offset,
        point_cell.reshape(run_count, cap),
        point_tile.reshape(run_count, cap),
    )


def solution(mesh):
    in_specs = (
        P(None, "gx", "gy", "gz"),
        P("gx", "gy", "gz"),
        P(None, ("gx", "gy", "gz")),
        P(None, ("gx", "gy", "gz")),
        P(("gx", "gy", "gz")),
        P(("gx", "gy", "gz"), None),
    )
    out_specs = (P(None, "gx", "gy", "gz"), P(None, ("gx", "gy", "gz")))
    return jax.shard_map(
        per_device, mesh=mesh, in_specs=in_specs, out_specs=out_specs, check_vma=False
    )
```

time: 67.2 us -> 75 us (1.12)
  Pallas kernels: 63.1 us -> 70.8 us
    pallas_call x1, Pallas kernels: 63.1 us -> 70.8 us  [per_device(): pl.pallas_call(functools.partial(kernel, sizes), out_shape=(jax.ShapeDtyp...]
where the time goes in v1:
time: 75 us; the launch traced here: 74.7 us
  Pallas kernels  70.8 us (94%)
  local copies, waits for them, and re-layouts  3.27 us (4%)
    pallas_call x1, Pallas kernels, per_device(): pl.pallas_call(functools.partial(kernel, sizes), out_shape=(jax.ShapeDtyp...  70.8 us
    unnamed x4, local copies, waits for them, and re-layouts  3.27 us

profile of v1, /device:TPU:0, one launch (start us, length us, event | category | flops | bytes accessed | tf_op | source)
XLA Modules:
  0.0 74.7 jit_solution(16950463562785281589)
XLA Ops:
  0.6 70.8 %farm_step.1 = (f32[3,64,16,128]{3,2,1,0:T(8,128)}, f32[3,1024]{1,0:T(4,128)}) custom-call(f32[3,64,16,128]{3,2,1,0:T(8,128)} %vel.1, f32[64,16,128]{2,1,0:T(8,128)} %visc_in.1, f32[3,1024]{1,0:T(4,128)} %force.1, f32[3,1024]{1,0:T(4,128)} %offset.1, s32[8,128]{1,0:T(8,128)} %bitcast.2, s32[8,128]{1,0:T(8,128)} %bitcast.3), custom_call_target="tpu_custom_call" | custom-call | tf_op jit(solution)/shard_map/farm_step/pallas_call | solution.py:522
  71.4 0.0 copy-start
  71.4 2.7 %copy.10 = f32[3,64,16,128]{3,2,1,0:T(8,128)} copy(f32[3,64,16,128]{3,2,1,0:T(8,128)} %get-tuple-element.4) | data formatting | bytes 3145728
  74.1 0.0 copy-done
  74.1 0.6 copy.11
Async XLA Ops:
  71.4 2.7 %copy-start = (f32[3,1024]{1,0:T(4,128)S(1)}, f32[3,1024]{1,0:T(4,128)}, u32[]{:S(2)}) copy-start(f32[3,1024]{1,0:T(4,128)} %get-tuple-element.5) | copy-start | bytes 36868

commit v2 on v0

--- a/solution.py
+++ b/solution.py
@@ -1,4 +1,5 @@
 import functools
+import math
 
 import jax
 import jax.numpy as jnp
@@ -13,6 +14,7 @@
 one_third = 1.0 / 3.0
 two_thirds = 2.0 / 3.0
 run_count = 8
+step_blocks = 6
 
 
 def split_by(x, n):
@@ -32,13 +34,13 @@
     middles = lax.broadcasted_iota(jnp.int32, (cells, centre.shape[1]), 0).astype(jnp.float32) + 0.5
     scaled = (middles - centre) / kernel_width
     unscaled = jnp.exp(-scaled * scaled)
-    return unscaled / jnp.sum(unscaled, axis=0, keepdims=True)
+    return unscaled * (1.0 / jnp.sum(unscaled, axis=0, keepdims=True))
 
 
 def kernel(
     sizes,
     vel,
-    visc,
+    visc_in,
     force,
     offset,
     cell,
@@ -46,6 +48,12 @@
     out_vel,
     out_pts,
     field,
+    visc,
+    fresh,
+    local_sem,
+    wx_kept,
+    wy_kept,
+    right_kept,
     force_acc,
     forcing,
     w_high,
@@ -93,6 +101,13 @@
         da, db, dc = step_of(n)
         return a + sign * da, b + sign * db, c + sign * dc
 
+    vel_copy = pltpu.make_async_copy(
+        vel, field.at[0, :, pl.ds(2, cx), pl.ds(8, cy)], local_sem.at[0]
+    )
+    vel_copy.start()
+    visc_copy = pltpu.make_async_copy(visc_in, visc, local_sem.at[1])
+    visc_copy.start()
+
     slots[...] = jnp.zeros_like(slots)
     returned[...] = jnp.zeros_like(returned)
     y_recv[...] = jnp.zeros_like(y_recv)
@@ -237,6 +252,7 @@
 
     first = lax.rem(a, 2)
     z_send[...] = jnp.zeros_like(z_send)
+    vel_copy.wait()
 
     for turn in range(2):
         h = first if turn == 0 else 1 - first
@@ -244,9 +260,7 @@
         def stage_in(g, carry):
             for t in range(4):
                 i = h * half_planes + 4 * g + t
-                v = [vel[comp, i] for comp in range(3)]
-                for comp in range(3):
-                    field[0, comp, i + 2, 8 : 8 + cy, :] = v[comp]
+                v = [field[0, comp, i + 2, 8 : 8 + cy, :] for comp in range(3)]
                 pack_plane(0, h, g, t, v)
             return carry
 
@@ -262,7 +276,7 @@
         span_of(p, count) for p, count in zip(where_am_i, counts)
     )
     blocks = in_a * in_b * in_c
-    pairs = (blocks + 1) // 2
+    steps = (blocks + step_blocks - 1) // step_blocks
 
     def block_of(v):
         n = (low_a + v // (in_b * in_c)) * 9 + (low_b + v // in_c % in_b) * 3 + low_c + v % in_c
@@ -279,17 +293,21 @@
 
     lax.fori_loop(0, 27, wait_points, 0)
 
-    def pair_slots(pair):
-        n0, n1 = block_of(2 * pair), block_of(2 * pair + 1)
-        return n0, n1, jnp.concatenate([slots[n0], slots[n1]], axis=1)
+    def blocks_of(step):
+        return [block_of(step_blocks * step + m) for m in range(step_blocks)]
 
     force_acc[...] = jnp.zeros_like(force_acc)
 
-    def spread(pair, carry):
-        _, _, s = pair_slots(pair)
+    def spread(step, carry):
+        s = jnp.concatenate([slots[n] for n in blocks_of(step)], axis=1)
         wx = weights(s[3:4], cx)
         wy = weights(s[4:5], cy)
         wz = weights(s[5:6], cz)
+        wx_kept[step] = wx
+        wy_kept[step] = wy
+        z_high, z_low = halves(wz)
+        for m, part in enumerate((z_high, z_high, z_low, z_low)):
+            right_kept[step, m * cz : (m + 1) * cz, :] = part
         a_high, a_low = halves(jnp.concatenate([s[d : d + 1] * wx for d in range(3)], axis=0))
         for j in range(cy):
             high, low = halves(wy[j : j + 1] * wz)
@@ -302,12 +320,18 @@
         )
         return carry
 
-    lax.fori_loop(0, pairs, spread, 0)
+    lax.fori_loop(0, steps, spread, 0)
 
     for j in range(cy):
         turned = force_acc[j * cz : (j + 1) * cz, :].T
         for comp in range(3):
             forcing[pl.ds(comp * cx * cy + j, cx, stride=cy), :] = turned[comp * cx : (comp + 1) * cx]
+
+    def out_copy(h):
+        span = pl.ds(h * half_planes, half_planes)
+        return pltpu.make_async_copy(fresh.at[:, span], out_vel.at[:, span], local_sem.at[2 + h])
+
+    visc_copy.wait()
 
     for s in range(3):
         for turn in range(2):
@@ -349,14 +373,14 @@
                         tend = nu * spreading - carried * (1.0 / 12.0) + forcing[pl.ds(row, cy), :]
                         moved = v + time_step * tend
                         if s == 1:
-                            moved = 0.75 * vel[comp, i] + 0.25 * moved
+                            moved = 0.75 * field[0, comp, i + 2, 8 : 8 + cy, :] + 0.25 * moved
                         elif s == 2:
-                            moved = one_third * vel[comp, i] + two_thirds * moved
+                            moved = one_third * field[0, comp, i + 2, 8 : 8 + cy, :] + two_thirds * moved
                         result.append(moved)
                         if s < 2:
                             field[s + 1, comp, i + 2, 8 : 8 + cy, :] = moved
                         else:
-                            out_vel[comp, i] = moved
+                            fresh[comp, i] = moved
                             high, low = halves(moved)
                             v_split[pl.ds(row, cy), 0:cz] = high
                             v_split[pl.ds(row, cy), cz : 2 * cz] = low
@@ -367,6 +391,8 @@
             lax.fori_loop(0, groups, advance, 0)
             if s < 2:
                 send_half(s + 1, h)
+            else:
+                out_copy(h).start()
 
     def ret_copy(n, place):
         return pltpu.make_async_remote_copy(
@@ -380,24 +406,22 @@
 
     sampled[...] = jnp.zeros_like(sampled)
 
-    def sample(pair, carry):
-        n0, n1, s = pair_slots(pair)
-        wx = weights(s[3:4], cx)
-        wy = weights(s[4:5], cy)
-        high, low = halves(weights(s[5:6], cz))
-        right = jnp.concatenate([high, high, low, low], axis=0)
+    def sample(step, carry):
+        places = blocks_of(step)
+        right = right_kept[step]
         for comp in range(3):
             v = v_split[comp * cx * cy : (comp + 1) * cx * cy, :]
-            product[...] = jnp.dot(
+            product[comp] = jnp.dot(
                 jnp.concatenate([v, v], axis=1), right, preferred_element_type=jnp.float32
             )
-            total = jnp.zeros((cy, 2 * cap), jnp.float32)
+        for comp in range(3):
+            total = jnp.zeros((cy, step_blocks * cap), jnp.float32)
             for i in range(cx):
-                total += wx[i : i + 1] * product[i * cy : (i + 1) * cy, :]
-            row = jnp.sum(total * wy, axis=0, keepdims=True)
-            sampled[n0, comp : comp + 1, :] = row[:, :cap]
-            sampled[n1, comp : comp + 1, :] = row[:, cap:]
-        for n in (n0, n1):
+                total += wx_kept[step, i : i + 1, :] * product[comp, i * cy : (i + 1) * cy, :]
+            row = jnp.sum(total * wy_kept[step], axis=0, keepdims=True)
+            for m, n in enumerate(places):
+                sampled[n, comp : comp + 1, :] = row[:, m * cap : (m + 1) * cap]
+        for n in places:
 
             @pl.when((n != 13) & (n < 27))
             def _():
@@ -405,7 +429,7 @@
 
         return carry
 
-    lax.fori_loop(0, pairs, sample, 0)
+    lax.fori_loop(0, steps, sample, 0)
     returned[13] = sampled[13]
 
     def wait_returned(n, carry):
@@ -438,6 +462,8 @@
     lax.fori_loop(0, 27, finish, 0)
     for s in range(3):
         wait_sends(s)
+    for h in range(2):
+        out_copy(h).wait()
 
 
 def per_device(velocity, viscosity, point_force, point_offset, point_cell, point_tile):
@@ -450,21 +476,31 @@
     f32, bf16 = jnp.float32, jnp.bfloat16
     dma = pltpu.SemaphoreType.DMA
     whole = pl.BlockSpec(memory_space=pltpu.VMEM)
+    anywhere = pl.BlockSpec(memory_space=pl.ANY)
+    most = math.prod(min(3, n) for n in mesh_sizes)
+    steps = -(-most // step_blocks)
+    width = step_blocks * cap
     return pl.pallas_call(
         functools.partial(kernel, sizes),
         out_shape=(
             jax.ShapeDtypeStruct(velocity.shape, f32),
             jax.ShapeDtypeStruct(point_force.shape, f32),
         ),
-        in_specs=[whole] * 6,
-        out_specs=(whole, whole),
+        in_specs=[anywhere] * 2 + [whole] * 4,
+        out_specs=(anywhere, whole),
         scratch_shapes=[
             pltpu.VMEM((3, 3, cx + 4, cy + 16, cz), f32),
+            pltpu.VMEM((cx, cy, cz), f32),
+            pltpu.VMEM((3, cx, cy, cz), f32),
+            dma((4,)),
+            pltpu.VMEM((steps, cx, width), f32),
+            pltpu.VMEM((steps, cy, width), f32),
+            pltpu.VMEM((steps, 4 * cz, width), bf16),
             pltpu.VMEM((cy * cz, 3 * cx), f32),
             pltpu.VMEM((3 * cx * cy, cz), f32),
-            pltpu.VMEM((cy * cz, 2 * cap), bf16),
-            pltpu.VMEM((cy * cz, 2 * cap), bf16),
-            pltpu.VMEM((cx * cy, 2 * cap), f32),
+            pltpu.VMEM((cy * cz, width), bf16),
+            pltpu.VMEM((cy * cz, width), bf16),
+            pltpu.VMEM((3, cx * cy, width), f32),
             pltpu.VMEM((3 * cx * cy, 2 * cz), bf16),
             pltpu.VMEM((run_count, 8, cap), f32),
             pltpu.VMEM((run_count, cap), jnp.int32),

time: 67.2 us -> 62.7 us (0.933)
  Pallas kernels: 63.1 us -> 58.5 us
    pallas_call x1, Pallas kernels: 63.1 us -> 58.5 us  [per_device(): pl.pallas_call(functools.partial(kernel, sizes), out_shape=(jax.ShapeDtyp...]
where the time goes in v2:
time: 62.7 us; the launch traced here: 62.4 us
  Pallas kernels  58.5 us (93%)
  local copies, waits for them, and re-layouts  3.27 us (5%)
  between operations  0.65 us (1%)
    pallas_call x1, Pallas kernels, per_device(): pl.pallas_call(functools.partial(kernel, sizes), out_shape=(jax.ShapeDtyp...  58.5 us
    unnamed x4, local copies, waits for them, and re-layouts  3.27 us

profile of v2, /device:TPU:0, one launch (start us, length us, event | category | flops | bytes accessed | tf_op | source)
XLA Modules:
  0.0 62.4 jit_solution(8769344247548147224)
XLA Ops:
  0.6 58.5 %farm_step.1 = (f32[3,64,16,128]{3,2,1,0:T(8,128)}, f32[3,1024]{1,0:T(4,128)}) custom-call(f32[3,64,16,128]{3,2,1,0:T(8,128)} %vel.1, f32[64,16,128]{2,1,0:T(8,128)} %visc_in.1, f32[3,1024]{1,0:T(4,128)} %force.1, f32[3,1024]{1,0:T(4,128)} %offset.1, s32[8,128]{1,0:T(8,128)} %bitcast.2, s32[8,128]{1,0:T(8,128)} %bitcast.3), custom_call_target="tpu_custom_call" | custom-call | tf_op jit(solution)/shard_map/farm_step/pallas_call | solution.py:483
  59.1 0.0 copy-start
  59.1 2.7 %copy.10 = f32[3,64,16,128]{3,2,1,0:T(8,128)} copy(f32[3,64,16,128]{3,2,1,0:T(8,128)} %get-tuple-element.4) | data formatting | bytes 3145728
  61.8 0.0 copy-done
  61.8 0.6 copy.11
Async XLA Ops:
  59.1 2.7 %copy-start = (f32[3,1024]{1,0:T(4,128)S(1)}, f32[3,1024]{1,0:T(4,128)}, u32[]{:S(2)}) copy-start(f32[3,1024]{1,0:T(4,128)} %get-tuple-element.5) | copy-start | bytes 36868

commit v3 on v1

--- a/solution.py
+++ b/solution.py
@@ -1,4 +1,5 @@
 import functools
+import math
 
 import jax
 import jax.numpy as jnp
@@ -13,6 +14,7 @@
 one_third = 1.0 / 3.0
 two_thirds = 2.0 / 3.0
 run_count = 8
+step_blocks = 6
 
 
 def split_by(x, n):
@@ -32,7 +34,7 @@
     middles = lax.broadcasted_iota(jnp.int32, (cells, centre.shape[1]), 0).astype(jnp.float32) + 0.5
     scaled = (middles - centre) / kernel_width
     unscaled = jnp.exp(-scaled * scaled)
-    return unscaled / jnp.sum(unscaled, axis=0, keepdims=True)
+    return unscaled * (1.0 / jnp.sum(unscaled, axis=0, keepdims=True))
 
 
 def kernel(
@@ -49,6 +51,11 @@
     visc,
     fresh,
     local_sem,
+    wx_kept,
+    wy_kept,
+    wz_kept,
+    force_kept,
+    right_kept,
     force_acc,
     forcing,
     w_high,
@@ -284,7 +291,7 @@
         span_of(p, count) for p, count in zip(where_am_i, counts)
     )
     blocks = in_a * in_b * in_c
-    pairs = (blocks + 1) // 2
+    steps = (blocks + step_blocks - 1) // step_blocks
 
     def block_of(v):
         n = (low_a + v // (in_b * in_c)) * 9 + (low_b + v // in_c % in_b) * 3 + low_c + v % in_c
@@ -301,10 +308,27 @@
 
     lax.fori_loop(0, 27, wait_points, 0)
 
-    def pair_slots(pair):
-        n0, n1 = block_of(2 * pair), block_of(2 * pair + 1)
-        return n0, n1, jnp.concatenate([slots[n0], slots[n1]], axis=1)
-
+    def blocks_of(step):
+        return [block_of(step_blocks * step + m) for m in range(step_blocks)]
+
+    def prepare(step, carry):
+        s = jnp.concatenate([slots[n] for n in blocks_of(step)], axis=1)
+        wx = weights(s[3:4], cx)
+        wz = weights(s[5:6], cz)
+        wx_kept[step] = wx
+        wy_kept[step] = weights(s[4:5], cy)
+        wz_kept[step] = wz
+        z_high, z_low = halves(wz)
+        for m, part in enumerate((z_high, z_high, z_low, z_low)):
+            right_kept[step, m * cz : (m + 1) * cz, :] = part
+        for d in range(3):
+            a_high, a_low = halves(s[d : d + 1] * wx)
+            for m, part in enumerate((a_high, a_low, a_high)):
+                force_kept[step, d * cx : (d + 1) * cx, m * width : (m + 1) * width] = part
+        return carry
+
+    width = step_blocks * cap
+    lax.fori_loop(0, steps, prepare, 0)
     force_acc[...] = jnp.zeros_like(force_acc)
     visc_copy.wait()
 
@@ -314,24 +338,21 @@
     def spread_half(turn):
         h = half_of(turn)
 
-        def spread(pair, carry):
-            _, _, s = pair_slots(pair)
-            wx = weights(s[3:4], cx)
-            wy = half_rows(weights(s[4:5], cy), h)
-            wz = weights(s[5:6], cz)
-            a_high, a_low = halves(jnp.concatenate([s[d : d + 1] * wx for d in range(3)], axis=0))
+        def spread(step, carry):
+            wy = half_rows(wy_kept[step], h)
+            wz = wz_kept[step]
             for j in range(rows):
                 high, low = halves(wy[j : j + 1] * wz)
                 w_high[j * cz : (j + 1) * cz, :] = high
                 w_low[j * cz : (j + 1) * cz, :] = low
-            right = jnp.concatenate([a_high, a_low, a_high], axis=1)
+            right = force_kept[step]
             left = jnp.concatenate([w_high[...], w_high[...], w_low[...]], axis=1)
             force_acc[turn] += lax.dot_general(
                 left, right, (((1,), (1,)), ((), ())), preferred_element_type=jnp.float32
             )
             return carry
 
-        lax.fori_loop(0, pairs, spread, 0)
+        lax.fori_loop(0, steps, spread, 0)
         for j in range(rows):
             turned = force_acc[turn, j * cz : (j + 1) * cz, :].T
             for comp in range(3):
@@ -440,26 +461,26 @@
     def sample_half(turn):
         h = half_of(turn)
 
-        def sample(pair, carry):
-            n0, n1, s = pair_slots(pair)
-            wx = weights(s[3:4], cx)
-            wy = half_rows(weights(s[4:5], cy), h)
-            high, low = halves(weights(s[5:6], cz))
-            right = jnp.concatenate([high, high, low, low], axis=0)
+        def sample(step, carry):
+            places = blocks_of(step)
+            v = v_split[turn]
+            product[...] = jnp.dot(
+                jnp.concatenate([v, v], axis=1), right_kept[step], preferred_element_type=jnp.float32
+            )
+            wy = half_rows(wy_kept[step], h)
             for comp in range(3):
-                v = v_split[turn, comp * cx * rows : (comp + 1) * cx * rows, :]
-                product[comp] = jnp.dot(
-                    jnp.concatenate([v, v], axis=1), right, preferred_element_type=jnp.float32
-                )
-            for comp in range(3):
-                total = jnp.zeros((rows, 2 * cap), jnp.float32)
+                total = jnp.zeros((rows, width), jnp.float32)
                 for i in range(cx):
-                    total += wx[i : i + 1] * product[comp, i * rows : (i + 1) * rows, :]
+                    start = (comp * cx + i) * rows
+                    total += wx_kept[step, i : i + 1, :] * product[start : start + rows, :]
                 row = jnp.sum(total * wy, axis=0, keepdims=True)
-                sampled[n0, comp : comp + 1, :] += row[:, :cap]
-                sampled[n1, comp : comp + 1, :] += row[:, cap:]
+                for m, n in enumerate(places):
+                    part = row[:, m * cap : (m + 1) * cap]
+                    if turn == 1:
+                        part = part + sampled[n, comp : comp + 1, :]
+                    sampled[n, comp : comp + 1, :] = part
             if turn == 1:
-                for n in (n0, n1):
+                for n in places:
 
                     @pl.when((n != 13) & (n < 27))
                     def _():
@@ -467,7 +488,7 @@
 
             return carry
 
-        lax.fori_loop(0, pairs, sample, 0)
+        lax.fori_loop(0, steps, sample, 0)
 
     sample_half(0)
     section(2, 1)
@@ -519,6 +540,9 @@
     dma = pltpu.SemaphoreType.DMA
     whole = pl.BlockSpec(memory_space=pltpu.VMEM)
     anywhere = pl.BlockSpec(memory_space=pl.ANY)
+    most = math.prod(min(3, n) for n in mesh_sizes)
+    steps = -(-most // step_blocks)
+    width = step_blocks * cap
     return pl.pallas_call(
         functools.partial(kernel, sizes),
         out_shape=(
@@ -532,11 +556,16 @@
             pltpu.VMEM((cx, cy, cz), f32),
             pltpu.VMEM((3, cx, cy, cz), f32),
             dma((4,)),
+            pltpu.VMEM((steps, cx, width), f32),
+            pltpu.VMEM((steps, cy, width), f32),
+            pltpu.VMEM((steps, cz, width), f32),
+            pltpu.VMEM((steps, 3 * cx, 3 * width), bf16),
+            pltpu.VMEM((steps, 4 * cz, width), bf16),
             pltpu.VMEM((2, rows * cz, 3 * cx), f32),
             pltpu.VMEM((2, 3 * cx * rows, cz), f32),
-            pltpu.VMEM((rows * cz, 2 * cap), bf16),
-            pltpu.VMEM((rows * cz, 2 * cap), bf16),
-            pltpu.VMEM((3, cx * rows, 2 * cap), f32),
+            pltpu.VMEM((rows * cz, width), bf16),
+            pltpu.VMEM((rows * cz, width), bf16),
+            pltpu.VMEM((3 * cx * rows, width), f32),
             pltpu.VMEM((2, 3 * cx * rows, 2 * cz), bf16),
             pltpu.VMEM((run_count, 8, cap), f32),
             pltpu.VMEM((run_count, cap), jnp.int32),

time: 75 us -> 67.8 us (0.904)
  Pallas kernels: 70.8 us -> 63.6 us
    pallas_call x1, Pallas kernels: 70.8 us -> 63.6 us  [per_device(): pl.pallas_call(functools.partial(kernel, sizes), out_shape=(jax.ShapeDtyp...]
where the time goes in v3:
time: 67.8 us; the launch traced here: 67.5 us
  Pallas kernels  63.6 us (94%)
  local copies, waits for them, and re-layouts  3.27 us (5%)
    pallas_call x1, Pallas kernels, per_device(): pl.pallas_call(functools.partial(kernel, sizes), out_shape=(jax.ShapeDtyp...  63.6 us
    unnamed x4, local copies, waits for them, and re-layouts  3.27 us

profile of v3, /device:TPU:0, one launch (start us, length us, event | category | flops | bytes accessed | tf_op | source)
XLA Modules:
  0.0 67.5 jit_solution(5927943023158158196)
XLA Ops:
  0.6 63.6 %farm_step.1 = (f32[3,64,16,128]{3,2,1,0:T(8,128)}, f32[3,1024]{1,0:T(4,128)}) custom-call(f32[3,64,16,128]{3,2,1,0:T(8,128)} %vel.1, f32[64,16,128]{2,1,0:T(8,128)} %visc_in.1, f32[3,1024]{1,0:T(4,128)} %force.1, f32[3,1024]{1,0:T(4,128)} %offset.1, s32[8,128]{1,0:T(8,128)} %bitcast.2, s32[8,128]{1,0:T(8,128)} %bitcast.3), custom_call_target="tpu_custom_call" | custom-call | tf_op jit(solution)/shard_map/farm_step/pallas_call | solution.py:546
  64.2 0.0 copy-start
  64.2 2.7 %copy.10 = f32[3,64,16,128]{3,2,1,0:T(8,128)} copy(f32[3,64,16,128]{3,2,1,0:T(8,128)} %get-tuple-element.4) | data formatting | bytes 3145728
  66.9 0.0 copy-done
  66.9 0.6 copy.11
Async XLA Ops:
  64.2 2.7 %copy-start = (f32[3,1024]{1,0:T(4,128)S(1)}, f32[3,1024]{1,0:T(4,128)}, u32[]{:S(2)}) copy-start(f32[3,1024]{1,0:T(4,128)} %get-tuple-element.5) | copy-start | bytes 36868
